TPU v7x, 768 devices: a whole 4x8x12 slice. The times are simulated.
768 devices in a mesh: wide: 12 (over z), rep: 16 (over y_hi, x, core), grp: 4 (over y_lo).
Axes of the slice: x: 4, y: 8 (y_hi: 2, y_lo: 4; y = y_hi * 4 + y_lo), z: 12, core: 2. Of those that a mesh axis runs over, the one named last changes fastest.
Arguments:
- features: bfloat16 [1536, 128, 128], P(('wide', 'grp'), 'rep'), may hold values from -6 to 6
- adjacency: bfloat16 [48, 16, 128, 48, 256], P(('wide', 'grp'), 'rep')
- slot_tile: int32 [48, 48], P(('wide', 'grp')), may hold values from 0 to 32, as said below
- in_degree: int32 [1536, 128], P(('wide', 'grp'), 'rep'), may hold values from 8 to 32
- w_self: bfloat16 [128, 512], replicated, may hold values from -0.5 to 0.5
- w_neigh: bfloat16 [128, 512], replicated, may hold values from -0.5 to 0.5
- bias: float32 [512], replicated, may hold values from -3 to 3
Outputs:
- embedding: bfloat16 [1536, 128, 512], P(('wide', 'grp'), 'rep')
Inputs may be any that keep to these rules, and one draw needn't show every extreme that they name: slot_tile[p, q] names a row tile of block p, or 32 for a slot that carries nothing; both kinds occur in every draw, and the share of empty slots differs from source block to source block.
All inputs are finite; a program needn't handle non-finite values.
Results may differ from a plain program's by a relative error of at most 0.011.
Values may be sent and summed in bfloat16 or wider, within the bound.
No kernel may reach another device: no remote copies, remote signals or barrier semaphores. Data moves between devices by JAX's collectives and lax.ppermute only.
A program may use at most 32 MiB of HBM per device.

v0:
```python
import jax
import jax.numpy as jnp
from jax import lax
from jax.sharding import PartitionSpec as P


def rounded_term(value):
    narrow = lax.optimization_barrier(value.astype(jnp.bfloat16))
    return narrow.astype(jnp.float32)


def local(features, adjacency, slot_tile, in_degree, w_self, w_neigh, bias):
    tiles, slice_rows, width = features.shape
    node_rows = features.reshape(tiles * slice_rows, width)
    tile_block = adjacency[0, 0]
    tile_rows, blocks, columns = tile_block.shape
    partial_value = jnp.dot(
        tile_block.reshape(tile_rows * blocks, columns),
        node_rows,
        preferred_element_type=jnp.float32,
    )
    partial_value = rounded_term(partial_value.reshape(tile_rows, blocks, width))
    summed_all = lax.psum(partial_value.astype(jnp.bfloat16), "rep").astype(jnp.float32)
    first_row = lax.axis_index("rep") * slice_rows
    my_share = lax.dynamic_slice_in_dim(summed_all, first_row, slice_rows, 0)
    my_share = my_share.astype(jnp.bfloat16)
    received = lax.all_to_all(my_share, ("wide", "grp"), split_axis=1, concat_axis=1, tiled=True)
    slot_ids = slot_tile[0]
    tile_ids = jnp.arange(tiles)
    select = (slot_ids[None, :] == tile_ids[:, None]).astype(jnp.bfloat16)
    neigh_sum = jnp.einsum("tq,iqf->tif", select, received, preferred_element_type=jnp.float32)
    aggregate = (neigh_sum / in_degree.astype(jnp.float32)[:, :, None]).astype(jnp.bfloat16)
    aggregate = aggregate.reshape(tiles * slice_rows, width)
    self_term = jnp.dot(node_rows, w_self, preferred_element_type=jnp.float32)
    neigh_term = jnp.dot(aggregate, w_neigh, preferred_element_type=jnp.float32)
    hidden_pre = self_term + neigh_term + bias
    embedding = jax.nn.relu(hidden_pre).astype(jnp.bfloat16)
    return embedding.reshape(tiles, slice_rows, w_self.shape[1])


def solution(mesh):
    return jax.shard_map(
        local,
        mesh=mesh,
        in_specs=(
            P(("wide", "grp"), "rep", None),
            P(("wide", "grp"), "rep", None, None, None),
            P(("wide", "grp"), None),
            P(("wide", "grp"), "rep"),
            P(),
            P(),
            P(),
        ),
        out_specs=P(("wide", "grp"), "rep", None),
        check_vma=False,
    )
```

profile of v0, /device:TPU:7, one launch (start us, length us, event | category | flops | bytes accessed | tf_op | source)
XLA Modules:
  0.0 247.9 jit_solution(16451626812642350277)
XLA Ops:
  6.5 0.0 copy-start
  6.5 0.0 copy-start.1
  6.5 0.0 copy-start.4
  6.5 0.0 copy-start.3
  6.5 0.0 copy-start.6
  6.5 0.0 copy-start.2
  6.6 0.0 copy-start.5
  6.6 0.0 all-reduce.2.cloned.1.call-start
  6.6 1.8 copy-done
  8.4 3.0 %fusion.2 = bf16[128,48,128]{2,1,0:T(8,128)(2,1)} fusion(bf16[1,1,128,48,256]{4,3,2,1,0:T(8,128)(2,1)S(1)} %copy-done, bf16[32,8,128]{2,1,0:T(8,128)(2,1)} %param.7), kind=kOutput, calls=%fused_computation.2 | convolution fusion | flops 403439616 | bytes 4784128 | tf_op jit(solution)/shard_map/dot_general | solution.py:17
  11.4 0.0 all-reduce.2.cloned.1.call-update
  11.4 199.8 %all-reduce.2.cloned.1.call-done = bf16[128,48,128]{2,1,0:T(8,128)(2,1)} async-done(((bf16[128,48,128]{2,1,0:T(8,128)(2,1)}), bf16[128,48,128]{2,1,0:T(8,128)(2,1)}) %all-reduce.2.cloned.1.call-update) | async-done | bytes 1572880 | tf_op jit(solution)/shard_map/psum | solution.py:23
  211.3 0.9 convert_convert_fusion
  212.2 0.7 copy.9
  212.8 13.6 %all-to-all-start = ((bf16[8,48,128]{2,0,1:T(8,128)(2,1)}), bf16[8,48,128]{2,0,1:T(8,128)(2,1)}, u32[]{:S(2)}, u32[]{:S(2)}) async-start(bf16[8,48,128]{2,0,1:T(8,128)(2,1)} %copy.9), calls=%async_computation | async-start | bytes 196608 | tf_op jit(solution)/shard_map/all_to_all | solution.py:27
  226.4 0.0 copy-done.4
  226.4 0.0 copy-done.1
  226.4 0.0 copy-done.3
  226.4 1.0 fusion.13
  227.4 10.6 %all-to-all-done = bf16[8,48,128]{2,0,1:T(8,128)(2,1)} async-done(((bf16[8,48,128]{2,0,1:T(8,128)(2,1)}), bf16[8,48,128]{2,0,1:T(8,128)(2,1)}, u32[]{:S(2)}, u32[]{:S(2)}) %all-to-all-start) | async-done | bytes 98336 | tf_op jit(solution)/shard_map/all_to_all | solution.py:27
  238.0 0.0 copy-done.6
  238.0 1.0 fusion.9
  239.0 0.0 copy-done.2
  239.0 0.0 copy-done.5
  239.1 2.0 fusion.8
  (1 shorter events, 0.0 us)
Async XLA Ops:
  6.5 1.9 copy-start
  6.5 219.9 %copy-start.1 = (bf16[32,8,128]{2,1,0:T(8,128)(2,1)S(1)}, bf16[32,8,128]{2,1,0:T(8,128)(2,1)}, u32[]{:S(2)}) copy-start(bf16[32,8,128]{2,1,0:T(8,128)(2,1)} %param.7) | copy-start | bytes 196612
  6.5 219.9 %copy-start.4 = (s32[32,8]{0,1:T(8,128)S(1)}, s32[32,8]{0,1:T(8,128)}, u32[]{:S(2)}) copy-start(s32[32,8]{0,1:T(8,128)} %param.10) | copy-start | bytes 3076
  6.5 219.9 %copy-start.3 = (bf16[128,512]{1,0:T(8,128)(2,1)S(1)}, bf16[128,512]{1,0:T(8,128)(2,1)}, u32[]{:S(2)}) copy-start(bf16[128,512]{1,0:T(8,128)(2,1)} %param.11) | copy-start | bytes 393220
  6.5 231.5 %copy-start.6 = (s32[1,48]{1,0:T(1,128)S(1)}, s32[1,48]{1,0:T(1,128)}, u32[]{:S(2)}) copy-start(s32[1,48]{1,0:T(1,128)} %param.9) | copy-start | bytes 580
  6.5 232.5 %copy-start.2 = (bf16[128,512]{1,0:T(8,128)(2,1)S(1)}, bf16[128,512]{1,0:T(8,128)(2,1)}, u32[]{:S(2)}) copy-start(bf16[128,512]{1,0:T(8,128)(2,1)} %param.12) | copy-start | bytes 393220
  6.6 232.5 %copy-start.5 = (f32[512]{0:T(512)S(1)}, f32[512]{0:T(512)}, u32[]{:S(2)}) copy-start(f32[512]{0:T(512)} %param.13) | copy-start | bytes 6148
  6.6 204.7 %all-reduce.2.cloned.1.call-start = ((), (), s32[]{:S(2)}) async-start(), calls=%async_computation.1 | async-start | bytes 3145728 | tf_op jit(solution)/shard_map/psum | solution.py:23
  212.8 25.2 %all-to-all-start = ((bf16[8,48,128]{2,0,1:T(8,128)(2,1)}), bf16[8,48,128]{2,0,1:T(8,128)(2,1)}, u32[]{:S(2)}, u32[]{:S(2)}) async-start(bf16[8,48,128]{2,0,1:T(8,128)(2,1)} %copy.9), calls=%async_computation | async-start | bytes 196608 | tf_op jit(solution)/shard_map/all_to_all | solution.py:27
Sparse Core Ops, SparseCore 0:
  11.5 199.6 all-reduce.1
where the time goes:
time: 248 us
  waiting for transfers between devices  210 us (85%)
  starting transfers between devices  13.6 us (5%)
  between operations  13.5 us (5%)
  matrix products  6.98 us (3%)
  local copies, waits for them, and re-layouts  2.52 us (1%)
    psum x1, waiting for transfers between devices, local(): lax.psum(partial_value.astype(jnp.bfloat16), 'rep').astype(jnp.float32)  200 us
    all_to_all x1, starting transfers between devices, local(): lax.all_to_all(my_share, ('wide', 'grp'), split_axis=1, concat_axis=1, ti...  13.6 us
    all_to_all x1, waiting for transfers between devices, local(): lax.all_to_all(my_share, ('wide', 'grp'), split_axis=1, concat_axis=1, ti...  10.6 us
  transfers between devices with their start and end apart: 2, of which 2 were waited for; matrix products, arithmetic and copies ran while one was open for 0% of the time, Pallas kernels for 0%

commit v1 on v0

v1 whole, which is shorter than its diff:
```python
import jax
import jax.numpy as jnp
from jax import lax
from jax.sharding import Mesh, PartitionSpec as P

YH, X, CORE = 2, 4, 2
AXES = ("z", "yh", "x", "core", "yl")
Y = ("yh", "yl")


def make_local(z, yl):
    def local(features, adjacency, slot_tile, in_degree, w_self, w_neigh, bias):
        tiles, s, f = features.shape
        node_rows = features.reshape(tiles * s, f)
        core = lax.axis_index("core")
        adj = adjacency.reshape(YH, X, CORE, s, z * yl, -1)

        def part(which):
            rows = lax.dynamic_index_in_dim(adj, which, 2, keepdims=False)
            return jnp.einsum("yxspc,cf->xyspf", rows, node_rows, preferred_element_type=jnp.float32)

        other = part(1 - core).astype(jnp.bfloat16)
        mine = part(core)
        got = lax.ppermute(other, "core", [(0, 1), (1, 0)])
        pair = (mine + got.astype(jnp.float32)).astype(jnp.bfloat16)
        got = lax.all_to_all(pair, "x", 0, 0, tiled=True)
        quad = jnp.sum(got.astype(jnp.float32), axis=0).astype(jnp.bfloat16)
        quad = quad.reshape(YH, s, z, yl, f).transpose(0, 3, 2, 1, 4).reshape(YH * yl, z, s, f)
        got = lax.all_to_all(quad, Y, 0, 0, tiled=True)
        full = jnp.sum(got.reshape(YH, yl, z, s, f).astype(jnp.float32), axis=0).astype(jnp.bfloat16)
        full = full.transpose(1, 0, 2, 3)
        received = lax.all_to_all(full, "z", 0, 0, tiled=True).reshape(z * yl, s, f)
        select = (slot_tile[0][None, :] == jnp.arange(tiles)[:, None]).astype(jnp.bfloat16)
        neigh_sum = jnp.einsum("tq,qsf->tsf", select, received, preferred_element_type=jnp.float32)
        aggregate = (neigh_sum / in_degree.astype(jnp.float32)[:, :, None]).astype(jnp.bfloat16)
        aggregate = aggregate.reshape(tiles * s, f)
        self_term = jnp.dot(node_rows, w_self, preferred_element_type=jnp.float32)
        neigh_term = jnp.dot(aggregate, w_neigh, preferred_element_type=jnp.float32)
        embedding = jax.nn.relu(self_term + neigh_term + bias).astype(jnp.bfloat16)
        return embedding.reshape(tiles, s, w_self.shape[1])

    return local


def solution(mesh):
    z, rep, yl = mesh.devices.shape
    fine = Mesh(mesh.devices.reshape(z, YH, X, CORE, yl), AXES)
    blocks, replicas = ("z", "yl"), ("yh", "x", "core")
    return jax.shard_map(
        make_local(z, yl),
        mesh=fine,
        in_specs=(
            P(blocks, replicas, None),
            P(blocks, replicas, None, None, None),
            P(blocks, None),
            P(blocks, replicas),
            P(),
            P(),
            P(),
        ),
        out_specs=P(blocks, replicas, None),
        check_vma=False,
    )
```

time: 248 us -> 74.6 us (0.30)
  the two profiles are of different devices: /device:TPU:7 before, /device:TPU:8 now
where the time goes in v1:
time: 74.6 us; the launch traced here: 74.2 us
  blocking collectives  36.6 us (49%)
  starting transfers between devices  13 us (17%)
  waiting for transfers between devices  12.3 us (16%)
  matrix products  8.02 us (11%)
  local copies, waits for them, and re-layouts  2.78 us (4%)
  other arithmetic  1.31 us (2%)
    all_to_all x1, blocking collectives, local(): got = lax.all_to_all(quad, Y, 0, 0, tiled=True)  19.8 us
    all_to_all x1, blocking collectives, local(): got = lax.all_to_all(pair, 'x', 0, 0, tiled=True)  16.8 us
    all_to_all x1, starting transfers between devices, local(): received = lax.all_to_all(full, 'z', 0, 0, tiled=True).reshape(z * yl, s, f)  11.1 us
    all_to_all x1, waiting for transfers between devices, local(): received = lax.all_to_all(full, 'z', 0, 0, tiled=True).reshape(z * yl, s, f)  9.7 us
    dot_general x2, matrix products, part(): jnp.einsum('yxspc,cf->xyspf', rows, node_rows, preferred_element_type=jnp...  4 us
    ppermute x1, waiting for transfers between devices, local(): got = lax.ppermute(other, 'core', [(0, 1), (1, 0)])  2.59 us
    dot_general x1, matrix products, local(): neigh_term = jnp.dot(aggregate, w_neigh, preferred_element_type=jnp.float32)  1.97 us
    unnamed x12, local copies, waits for them, and re-layouts  1.91 us
  transfers between devices with their start and end apart: 2, of which 2 were waited for; matrix products, arithmetic and copies ran while one was open for 3% of the time, Pallas kernels for 0%

profile of v1, /device:TPU:8, one launch (start us, length us, event | category | flops | bytes accessed | tf_op | source)
XLA Modules:
  0.0 74.2 jit_solution(13270931653200472472)
XLA Ops:
  0.0 0.0 copy-start
  0.0 0.0 copy-start.1
  0.0 1.9 %copy-done = bf16[1,1,128,48,256]{4,3,2,1,0:T(8,128)(2,1)S(1)} copy-done((bf16[1,1,128,48,256]{4,3,2,1,0:T(8,128)(2,1)S(1)}, bf16[1,1,128,48,256]{4,3,2,1,0:T(8,128)(2,1)}, u32[]{:S(2)}) %copy-start) | copy-done | bytes 3145752
  1.9 2.3 %fusion.12 = bf16[4,2,8,48,128]{4,3,2,0,1:T(8,128)(2,1)} fusion(bf16[2,4,2,8,48,256]{5,4,3,2,1,0:T(8,128)(2,1)S(1)} %bitcast.53, s32[]{:T(128)S(6)} %select_n.8, bf16[32,8,128]{2,1,0:T(8,128)(2,1)} %param.7), kind=kOutput, calls=%fused_computation.9 | convolution fusion | flops 201719808 | bytes 2424836 | tf_op jit(solution)/shard_map/yxspc,cf->xyspf/dot_general | solution.py:20
  4.2 1.9 %collective-permute-start = (bf16[4,2,8,48,128]{4,3,2,0,1:T(8,128)(2,1)}, bf16[4,2,8,48,128]{4,3,2,0,1:T(8,128)(2,1)}, u32[]{:S(2)}, u32[]{:S(2)}) collective-permute-start(bf16[4,2,8,48,128]{4,3,2,0,1:T(8,128)(2,1)} %fusion.12), channel_id=1, source_target_pairs={{0,4},{4,0},{1,5},{5,1},{2,6},{6,2},{3,7},{7,3},{8,12},{12,8},{9,1... | collective-permute-start | bytes 2359304 | tf_op jit(solution)/shard_map/ppermute | solution.py:24
  6.1 2.6 %collective-permute-done = bf16[4,2,8,48,128]{4,3,2,0,1:T(8,128)(2,1)} collective-permute-done((bf16[4,2,8,48,128]{4,3,2,0,1:T(8,128)(2,1)}, bf16[4,2,8,48,128]{4,3,2,0,1:T(8,128)(2,1)}, u32[]{:S(2)}, u32[]{:S(2)}) %collective-permute-start) | collective-permute-done | bytes 786464 | tf_op jit(solution)/shard_map/ppermute | solution.py:24
  8.7 0.0 copy-done.1
  8.7 1.7 %fusion.4 = bf16[4,2,8,48,128]{4,3,2,0,1:T(8,128)(2,1)S(1)} fusion(bf16[4,2,8,48,128]{4,3,2,0,1:T(8,128)(2,1)} %collective-permute-done, bf16[2,4,2,8,48,256]{5,4,3,2,1,0:T(8,128)(2,1)S(1)} %bitcast.54, s32[]{:T(128)S(6)} %select_n.7, bf16[32,8,128]{2,1,0:T(8,128)(2,1)S(1)} %copy-done.1), kind=kOutput, calls=%fused_computation.5 | convolution fusion | flops 202506240 | bytes 3211268 | tf_op jit(solution)/shard_map/yxspc,cf->xyspf/dot_general | solution.py:20
  10.4 0.1 copy.19
  10.5 16.8 %all_to_all.15 = bf16[4,2,8,48,128]{4,3,2,1,0:T(8,128)(2,1)} all-to-all(bf16[4,2,8,48,128]{4,3,2,1,0:T(8,128)(2,1)S(1)} %copy.19), channel_id=1, replica_groups=mesh['z'=12,'yh'=2,'x'=4,'core'=2,'yl'=4] {'x'}, dimensions={0} | all-to-all | bytes 1572864 | tf_op jit(solution)/shard_map/all_to_all | solution.py:26
  27.3 0.0 copy-start.3
  27.3 1.3 %reduce_sum.24 = bf16[2,8,48,128]{3,2,1,0:T(8,128)(2,1)S(1)} reduce(bf16[4,2,8,48,128]{4,3,2,1,0:T(8,128)(2,1)} %all_to_all.15, bf16[]{:T(256)} %constant.23.clone.1), dimensions={0}, to_apply=%region_0.1 | reduce | flops 294912 | bytes 983042 | tf_op jit(solution)/shard_map/reduce_sum | solution.py:27
  28.5 0.0 copy-start.5
  28.5 0.0 copy-start.4
  28.6 0.1 copy.21
  28.7 19.8 %all_to_all.16 = bf16[8,12,8,128]{3,2,1,0:T(8,128)(2,1)S(1)} all-to-all(bf16[8,12,8,128]{3,2,1,0:T(8,128)(2,1)S(1)} %bitcast.57), channel_id=1, replica_groups=mesh['z'=12,'yh'=2,'x'=4,'core'=2,'yl'=4] {'yh','yl'}, dimensions={0} | all-to-all | bytes 393216 | tf_op jit(solution)/shard_map/all_to_all | solution.py:29
  48.5 0.7 copy.23
  49.2 0.0 copy-start.2
  49.2 11.1 %all-to-all-start.2 = ((bf16[12,4,8,128]{3,1,2,0:T(4,128)(2,1)}), bf16[12,4,8,128]{3,1,2,0:T(4,128)(2,1)S(1)}, u32[]{:S(2)}, u32[]{:S(2)}) async-start(bf16[12,4,8,128]{3,1,2,0:T(4,128)(2,1)} %copy.23), calls=%async_computation.2 | async-start | bytes 196608 | tf_op jit(solution)/shard_map/all_to_all | solution.py:32
  60.3 0.0 copy-done.3
  60.4 1.9 %fusion.23 = f32[256,512]{1,0:T(8,128)} fusion(bf16[128,512]{1,0:T(8,128)(2,1)} %param.11, bf16[32,8,128]{2,1,0:T(8,128)(2,1)S(1)} %copy-done.1), kind=kOutput, calls=%fused_computation.20 | convolution fusion | flops 33554432 | bytes 720896 | tf_op jit(solution)/shard_map/dot_general | solution.py:37
  62.3 9.7 %all-to-all-done.2 = bf16[12,4,8,128]{3,1,2,0:T(4,128)(2,1)S(1)} async-done(((bf16[12,4,8,128]{3,1,2,0:T(4,128)(2,1)}), bf16[12,4,8,128]{3,1,2,0:T(4,128)(2,1)S(1)}, u32[]{:S(2)}, u32[]{:S(2)}) %all-to-all-start.2) | async-done | bytes 98336 | tf_op jit(solution)/shard_map/all_to_all | solution.py:32
  72.0 0.0 copy-done.5
  72.0 0.1 fusion.19
  72.2 0.0 copy-done.4
  72.2 0.0 copy-done.2
  72.2 2.0 %fusion.18 = bf16[32,8,512]{2,1,0:T(8,128)(2,1)} fusion(f32[256,512]{1,0:T(8,128)} %fusion.23, bf16[128,512]{1,0:T(8,128)(2,1)S(1)} %copy-done.2, f32[512]{0:T(512)S(1)} %copy-done.4, bf16[32,8,128]{2,0,1:T(8,128)(2,1)S(1)} %fusion.19), kind=kOutput, calls=%fused_computation.14 | convolution fusion | flops 34078720 | bytes 985088 | tf_op jit(solution)/shard_map/dot_general | solution.py:38
  (4 shorter events, 0.1 us)
Async XLA Ops:
  0.0 1.9 %copy-start = (bf16[1,1,128,48,256]{4,3,2,1,0:T(8,128)(2,1)S(1)}, bf16[1,1,128,48,256]{4,3,2,1,0:T(8,128)(2,1)}, u32[]{:S(2)}) copy-start(bf16[1,1,128,48,256]{4,3,2,1,0:T(8,128)(2,1)} %param.8) | copy-start | bytes 9437188
  0.0 8.7 %copy-start.1 = (bf16[32,8,128]{2,1,0:T(8,128)(2,1)S(1)}, bf16[32,8,128]{2,1,0:T(8,128)(2,1)}, u32[]{:S(2)}) copy-start(bf16[32,8,128]{2,1,0:T(8,128)(2,1)} %param.7) | copy-start | bytes 196612
  4.2 4.5 %collective-permute-start = (bf16[4,2,8,48,128]{4,3,2,0,1:T(8,128)(2,1)}, bf16[4,2,8,48,128]{4,3,2,0,1:T(8,128)(2,1)}, u32[]{:S(2)}, u32[]{:S(2)}) collective-permute-start(bf16[4,2,8,48,128]{4,3,2,0,1:T(8,128)(2,1)} %fusion.12), channel_id=1, source_target_pairs={{0,4},{4,0},{1,5},{5,1},{2,6},{6,2},{3,7},{7,3},{8,12},{12,8},{9,1... | collective-permute-start | bytes 2359304 | tf_op jit(solution)/shard_map/ppermute | solution.py:24
  27.3 33.1 %copy-start.3 = (s32[32,8]{0,1:T(8,128)S(1)}, s32[32,8]{0,1:T(8,128)}, u32[]{:S(2)}) copy-start(s32[32,8]{0,1:T(8,128)} %param.10) | copy-start | bytes 3076
  28.5 43.5 %copy-start.5 = (s32[1,48]{1,0:T(1,128)S(1)}, s32[1,48]{1,0:T(1,128)}, u32[]{:S(2)}) copy-start(s32[1,48]{1,0:T(1,128)} %param.9) | copy-start | bytes 580
  28.5 43.6 %copy-start.4 = (f32[512]{0:T(512)S(1)}, f32[512]{0:T(512)}, u32[]{:S(2)}) copy-start(f32[512]{0:T(512)} %param.13) | copy-start | bytes 6148
  49.2 23.0 %copy-start.2 = (bf16[128,512]{1,0:T(8,128)(2,1)S(1)}, bf16[128,512]{1,0:T(8,128)(2,1)}, u32[]{:S(2)}) copy-start(bf16[128,512]{1,0:T(8,128)(2,1)} %param.12) | copy-start | bytes 393220
  49.2 22.8 %all-to-all-start.2 = ((bf16[12,4,8,128]{3,1,2,0:T(4,128)(2,1)}), bf16[12,4,8,128]{3,1,2,0:T(4,128)(2,1)S(1)}, u32[]{:S(2)}, u32[]{:S(2)}) async-start(bf16[12,4,8,128]{3,1,2,0:T(4,128)(2,1)} %copy.23), calls=%async_computation.2 | async-start | bytes 196608 | tf_op jit(solution)/shard_map/all_to_all | solution.py:32

commit v2 on v1

v2 whole, which is shorter than its diff:
```python
import functools

import jax
import jax.numpy as jnp
from jax import lax
from jax.experimental import pallas as pl
from jax.experimental.pallas import tpu as pltpu
from jax.sharding import Mesh, PartitionSpec as P

YH, X, CORE = 2, 4, 2
AXES = ("z", "yh", "x", "core", "yl")
VMEM = pl.BlockSpec(memory_space=pltpu.VMEM)
PARAMS = pltpu.CompilerParams(vmem_limit_bytes=32 * 1024 * 1024)


def multiply_half(which, features_ref, adjacency_ref, out_ref):
    s, p, c = adjacency_ref.shape[3:]
    right = features_ref[...].astype(jnp.bfloat16)
    for a in range(X):
        for b in range(YH):
            left = adjacency_ref[b, a, which].reshape(s * p, c)
            out_ref[a, b] = jnp.dot(left, right, preferred_element_type=jnp.float32).astype(jnp.bfloat16)


def other_kernel(features_ref, adjacency_ref, out_ref):
    multiply_half(1 - lax.axis_index("core"), features_ref, adjacency_ref, out_ref)


def own_kernel(features_ref, adjacency_ref, slot_ref, in_degree_ref, out_ref, select_ref, degree_ref):
    multiply_half(lax.axis_index("core"), features_ref, adjacency_ref, out_ref)
    rows, wide = select_ref.shape
    s, tiles = in_degree_ref.shape
    p = slot_ref.shape[1]
    column = lax.broadcasted_iota(jnp.int32, (p, wide), 1)
    source = lax.rem(lax.div(column, s), p)
    spread = (source == lax.broadcasted_iota(jnp.int32, (p, wide), 0)).astype(jnp.float32).astype(jnp.bfloat16)
    slots = slot_ref[...].astype(jnp.float32).astype(jnp.bfloat16)
    slots = jnp.dot(slots, spread, preferred_element_type=jnp.float32).astype(jnp.int32)
    wanted = slots * s + lax.rem(lax.broadcasted_iota(jnp.int32, (1, wide), 1), s)
    ids = lax.broadcasted_iota(jnp.int32, (rows, wide), 0)
    select_ref[...] = (wanted == ids).astype(jnp.float32).astype(jnp.bfloat16)
    row = lax.broadcasted_iota(jnp.int32, (rows, s), 0)
    pick = (lax.rem(row, s) == lax.broadcasted_iota(jnp.int32, (rows, s), 1)).astype(jnp.float32)
    degrees = in_degree_ref[...].astype(jnp.float32).astype(jnp.bfloat16)
    degrees = jnp.dot(pick.astype(jnp.bfloat16), degrees, preferred_element_type=jnp.float32)
    tile = lax.div(lax.broadcasted_iota(jnp.int32, (rows, tiles), 0), s)
    mine = tile == lax.broadcasted_iota(jnp.int32, (rows, tiles), 1)
    degree = jnp.sum(jnp.where(mine, degrees, 0.0), axis=1, keepdims=True)
    degree_ref[...] = jnp.broadcast_to(degree, degree_ref.shape)


def half_call(kernel, operands, extra):
    node_rows, adj = operands[:2]
    _, _, _, s, p, c = adj.shape
    f = node_rows.shape[1]
    return pl.pallas_call(
        kernel,
        out_shape=[jax.ShapeDtypeStruct((X, YH, s * p, f), jnp.bfloat16)] + extra,
        in_specs=[VMEM] * len(operands),
        out_specs=[VMEM] * (1 + len(extra)),
        compiler_params=PARAMS,
        cost_estimate=pl.CostEstimate(flops=X * YH * s * p * c * f * 2, bytes_accessed=3000000, transcendentals=0),
    )(*operands)


def pair_kernel(mine_ref, got_ref, out_ref):
    out_ref[...] = mine_ref[...] + got_ref[...]


def pair_sum(mine, got):
    return pl.pallas_call(
        pair_kernel,
        out_shape=jax.ShapeDtypeStruct(mine.shape, jnp.bfloat16),
        in_specs=[VMEM, VMEM],
        out_specs=VMEM,
        compiler_params=PARAMS,
    )(mine, got)


def quad_kernel(s, p, pieces_ref, out_ref, total):
    for b in range(YH):
        for i in range(s):
            at = pl.ds(i * p, p)
            acc = pieces_ref[0, b, at, :].astype(jnp.float32)
            for k in range(1, X):
                acc = acc + pieces_ref[k, b, at, :].astype(jnp.float32)
            total[b, at, :] = acc
    for b in range(YH):
        for q in range(p):
            out_ref[b * p + q] = total[b, pl.ds(q, s, stride=p), :].astype(jnp.bfloat16)


def quad_sum(pieces, s, p):
    f = pieces.shape[-1]
    return pl.pallas_call(
        functools.partial(quad_kernel, s, p),
        out_shape=jax.ShapeDtypeStruct((YH * p, s, f), jnp.bfloat16),
        in_specs=[VMEM],
        out_specs=VMEM,
        scratch_shapes=[pltpu.VMEM((YH, s * p, f), jnp.float32)],
        compiler_params=PARAMS,
    )(pieces)


def final_kernel(select_ref, degree_ref, features_ref, received_ref, w_self_ref, w_neigh_ref, bias_ref, out_ref):
    neigh_sum = jnp.dot(select_ref[...], received_ref[...], preferred_element_type=jnp.float32)
    aggregate = (neigh_sum / degree_ref[...]).astype(jnp.bfloat16)
    hidden = jnp.dot(features_ref[...].astype(jnp.bfloat16), w_self_ref[...], preferred_element_type=jnp.float32)
    hidden = hidden + jnp.dot(aggregate, w_neigh_ref[...], preferred_element_type=jnp.float32)
    out_ref[...] = jnp.maximum(hidden + bias_ref[...], 0.0).astype(jnp.bfloat16)


def make_local(z, yl):
    def local(features, adjacency, slot_tile, in_degree, w_self, w_neigh, bias):
        tiles, s, f = features.shape
        p = z * yl
        rows = tiles * s
        h = w_self.shape[1]
        node_rows = features.reshape(rows, f).astype(jnp.float32)
        adj = adjacency.reshape(YH, X, CORE, s, p, -1)
        (other,) = half_call(other_kernel, (node_rows, adj), [])
        got = lax.ppermute(other, "core", [(0, 1), (1, 0)])
        tables = [
            jax.ShapeDtypeStruct((rows, YH * p * s), jnp.bfloat16),
            jax.ShapeDtypeStruct((rows, f), jnp.float32),
        ]
        mine, select, degree = half_call(own_kernel, (node_rows, adj, slot_tile, in_degree.T), tables)
        pair = pair_sum(mine, got)
        quad = quad_sum(lax.all_to_all(pair, "x", 0, 0, tiled=True), s, p)
        received = lax.all_to_all(quad, ("yh", "z", "yl"), 0, 0, tiled=True)
        embedding = pl.pallas_call(
            final_kernel,
            out_shape=jax.ShapeDtypeStruct((rows, h), jnp.bfloat16),
            in_specs=[VMEM] * 7,
            out_specs=VMEM,
            compiler_params=PARAMS,
        )(select, degree, node_rows, received.reshape(YH * p * s, f), w_self, w_neigh, bias.reshape(1, h))
        return embedding.reshape(tiles, s, h)

    return local


def solution(mesh):
    z, rep, yl = mesh.devices.shape
    fine = Mesh(mesh.devices.reshape(z, YH, X, CORE, yl), AXES)
    blocks, replicas = ("z", "yl"), ("yh", "x", "core")
    return jax.shard_map(
        make_local(z, yl),
        mesh=fine,
        in_specs=(
            P(blocks, replicas, None),
            P(blocks, replicas, None, None, None),
            P(blocks, None),
            P(blocks, replicas),
            P(),
            P(),
            P(),
        ),
        out_specs=P(blocks, replicas, None),
        check_vma=False,
    )
```

time: 74.6 us -> 63.6 us (0.85)
  blocking collectives: 36.6 us -> 54.2 us
  starting transfers between devices: 13 us -> 1.92 us
  waiting for transfers between devices: 12.3 us -> 1.43 us
  matrix products: 8.02 us -> 0 us
  Pallas kernels: 0 us -> 2.89 us
  local copies, waits for them, and re-layouts: 2.78 us -> 1.91 us
    all_to_all x2, blocking collectives: 36.6 us -> 54.2 us  [the longest x1 37.5 us: local(): received = lax.all_to_all(quad, ('yh', 'z', 'yl'), 0, 0, tiled=True)]
    all_to_all x1 -> x0, starting transfers between devices: 11.1 us -> none  [local(): received = lax.all_to_all(full, 'z', 0, 0, tiled=True).reshape(z * yl, s, f)]
    all_to_all x1 -> x0, waiting for transfers between devices: 9.7 us -> none  [local(): received = lax.all_to_all(full, 'z', 0, 0, tiled=True).reshape(z * yl, s, f)]
    dot_general x5 -> x0, matrix products: 8.02 us -> none  [the longest x2 4 us: part(): jnp.einsum('yxspc,cf->xyspf', rows, node_rows, preferred_element_type=jnp...]
    pallas_call x0 -> x5, Pallas kernels: none -> 2.89 us  [the longest x2 1.33 us: half_call(): pl.pallas_call(kernel, out_shape=[jax.ShapeDtypeStruct((X, YH, s * p, f),...]
    reduce_sum x2 -> x0, other arithmetic: 1.3 us -> none  [the longest x1 1.27 us: local(): quad = jnp.sum(got.astype(jnp.float32), axis=0).astype(jnp.bfloat16)]
    ppermute x1, waiting for transfers between devices: 2.59 us -> 1.43 us  [local(): got = lax.ppermute(other, 'core', [(0, 1), (1, 0)])]
    convert_element_type x1, other arithmetic: 0.01 us -> 0.88 us  [local(): node_rows = features.reshape(rows, f).astype(jnp.float32)]
  transfers between devices with their start and end apart: 2 -> 1, of which waited for: 2 -> 1; matrix products, arithmetic and copies ran while one was open for 3% -> 0% of each run, Pallas kernels for 0% -> 1%
where the time goes in v2:
time: 63.6 us; the launch traced here: 63.3 us
  blocking collectives  54.2 us (85%)
  Pallas kernels  2.89 us (5%)
  starting transfers between devices  1.92 us (3%)
  local copies, waits for them, and re-layouts  1.91 us (3%)
  waiting for transfers between devices  1.43 us (2%)
  other arithmetic  0.88 us (1%)
    all_to_all x1, blocking collectives, local(): received = lax.all_to_all(quad, ('yh', 'z', 'yl'), 0, 0, tiled=True)  37.5 us
    all_to_all x1, blocking collectives, local(): quad = quad_sum(lax.all_to_all(pair, 'x', 0, 0, tiled=True), s, p)  16.7 us
    ppermute x1, starting transfers between devices, local(): got = lax.ppermute(other, 'core', [(0, 1), (1, 0)])  1.92 us
    unnamed x12, local copies, waits for them, and re-layouts  1.91 us
    ppermute x1, waiting for transfers between devices, local(): got = lax.ppermute(other, 'core', [(0, 1), (1, 0)])  1.43 us
    pallas_call x2, Pallas kernels, half_call(): pl.pallas_call(kernel, out_shape=[jax.ShapeDtypeStruct((X, YH, s * p, f),...  1.33 us
  transfers between devices with their start and end apart: 1, of which 1 were waited for; matrix products, arithmetic and copies ran while one was open for 0% of the time, Pallas kernels for 1%

profile of v2, /device:TPU:8, one launch (start us, length us, event | category | flops | bytes accessed | tf_op | source)
XLA Modules:
  0.0 63.3 jit_solution(9003126924171033311)
XLA Ops:
  0.0 0.0 copy-start.3
  0.0 0.0 copy-start.5
  0.0 0.9 %bitcast_convert_fusion.features_ref = f32[256,128]{1,0:T(8,128)S(1)} fusion(bf16[32,8,128]{2,1,0:T(8,128)(2,1)} %param.7), kind=kLoop, calls=%fused_computation | loop fusion | flops 32768 | bytes 196608 | tf_op jit(solution)/shard_map/convert_element_type | solution.py:119
  0.9 0.0 copy-start
  0.9 1.9 %copy-done = bf16[1,1,128,48,256]{4,3,2,1,0:T(8,128)(2,1)S(1)} copy-done((bf16[1,1,128,48,256]{4,3,2,1,0:T(8,128)(2,1)S(1)}, bf16[1,1,128,48,256]{4,3,2,1,0:T(8,128)(2,1)}, u32[]{:S(2)}) %copy-start) | copy-done | bytes 3145752
  2.8 0.6 shard_map.74
  3.4 1.9 %collective-permute-start = (bf16[4,2,384,128]{3,2,1,0:T(8,128)(2,1)S(1)}, bf16[4,2,384,128]{3,2,1,0:T(8,128)(2,1)S(1)}, u32[]{:S(2)}, u32[]{:S(2)}) collective-permute-start(bf16[4,2,384,128]{3,2,1,0:T(8,128)(2,1)S(1)} %shard_map.74), channel_id=1, source_target_pairs={{0,4},{4,0},{1,5},{5,1},{2,6},{6,2},{3,7},{7,3},{8,12},{12,8},{9,1... | collective-permute-start | bytes 2359304 | tf_op jit(solution)/shard_map/ppermute | solution.py:122
  5.3 0.0 copy-done.3
  5.3 0.0 copy-done.5
  5.3 0.8 %shard_map.73 = (bf16[4,2,384,128]{3,2,1,0:T(8,128)(2,1)S(1)}, bf16[256,768]{1,0:T(8,128)(2,1)S(1)}, f32[256,128]{1,0:T(8,128)S(1)}) custom-call(f32[256,128]{1,0:T(8,128)S(1)} %bitcast_convert_fusion.features_ref, bf16[2,4,2,8,48,256]{5,4,3,2,1,0:T(8,128)(2,1)S(1)} %bitcast.9, s32[1,48]{1,0:T(1,128)S(1)} %copy-done.5, s32[8,32]{1,0:T(8,128)S(1)} %bitcast.11), custom_call_target="tpu_custom_call" | custom-call | flops 201326592 | bytes 3000000 | tf_op jit(solution)/shard_map/pallas_call | solution.py:56
  6.1 0.0 copy-start.1
  6.1 0.0 copy-start.2
  6.1 0.0 copy-start.4
  6.1 1.4 %collective-permute-done.got_ref = bf16[4,2,384,128]{3,2,1,0:T(8,128)(2,1)S(1)} collective-permute-done((bf16[4,2,384,128]{3,2,1,0:T(8,128)(2,1)S(1)}, bf16[4,2,384,128]{3,2,1,0:T(8,128)(2,1)S(1)}, u32[]{:S(2)}, u32[]{:S(2)}) %collective-permute-start) | collective-permute-done | bytes 786464 | tf_op jit(solution)/shard_map/ppermute | solution.py:122
  7.5 0.2 shard_map.75
  7.7 16.7 %all_to_all.10.pieces_ref = bf16[4,2,384,128]{3,2,1,0:T(8,128)(2,1)S(1)} all-to-all(bf16[4,2,384,128]{3,2,1,0:T(8,128)(2,1)S(1)} %shard_map.75), channel_id=1, replica_groups=mesh['z'=12,'yh'=2,'x'=4,'core'=2,'yl'=4] {'x'}, dimensions={0} | all-to-all | bytes 1572864 | tf_op jit(solution)/shard_map/all_to_all | solution.py:129
  24.4 0.2 shard_map.76
  24.6 37.5 %all_to_all.11 = bf16[96,8,128]{2,1,0:T(8,128)(2,1)S(1)} all-to-all(bf16[96,8,128]{2,1,0:T(8,128)(2,1)S(1)} %shard_map.76), channel_id=1, replica_groups=mesh['z'=12,'yh'=2,'x'=4,'core'=2,'yl'=4] {'yh','z','yl'}, dimensions={0} | all-to-all | bytes 393216 | tf_op jit(solution)/shard_map/all_to_all | solution.py:130
  62.1 0.0 copy-done.1
  62.1 0.0 copy-done.2
  62.1 0.0 copy-done.4
  62.1 1.2 %shard_map.77 = bf16[256,512]{1,0:T(8,128)(2,1)} custom-call(bf16[256,768]{1,0:T(8,128)(2,1)S(1)} %get-tuple-element.8.select_ref, f32[256,128]{1,0:T(8,128)S(1)} %get-tuple-element.9.degree_ref, f32[256,128]{1,0:T(8,128)S(1)} %bitcast_convert_fusion.features_ref, bf16[768,128]{1,0:T(8,128)(2,1)S(1)} %bitcast.10, bf16[128,512]{1,0:T(8,128)(2,1)S(1)} %copy-done.1, ...), custom_call_target="tpu_custom_call" | custom-call | tf_op jit(solution)/shard_map/pallas_call | solution.py:131
Async XLA Ops:
  0.0 5.3 %copy-start.3 = (s32[32,8]{0,1:T(8,128)S(1)}, s32[32,8]{0,1:T(8,128)}, u32[]{:S(2)}) copy-start(s32[32,8]{0,1:T(8,128)} %param.10) | copy-start | bytes 3076
  0.0 5.3 %copy-start.5 = (s32[1,48]{1,0:T(1,128)S(1)}, s32[1,48]{1,0:T(1,128)}, u32[]{:S(2)}) copy-start(s32[1,48]{1,0:T(1,128)} %slot_ref.1) | copy-start | bytes 580
  0.9 1.9 %copy-start = (bf16[1,1,128,48,256]{4,3,2,1,0:T(8,128)(2,1)S(1)}, bf16[1,1,128,48,256]{4,3,2,1,0:T(8,128)(2,1)}, u32[]{:S(2)}) copy-start(bf16[1,1,128,48,256]{4,3,2,1,0:T(8,128)(2,1)} %param.8) | copy-start | bytes 9437188
  3.4 4.2 %collective-permute-start = (bf16[4,2,384,128]{3,2,1,0:T(8,128)(2,1)S(1)}, bf16[4,2,384,128]{3,2,1,0:T(8,128)(2,1)S(1)}, u32[]{:S(2)}, u32[]{:S(2)}) collective-permute-start(bf16[4,2,384,128]{3,2,1,0:T(8,128)(2,1)S(1)} %shard_map.74), channel_id=1, source_target_pairs={{0,4},{4,0},{1,5},{5,1},{2,6},{6,2},{3,7},{7,3},{8,12},{12,8},{9,1... | collective-permute-start | bytes 2359304 | tf_op jit(solution)/shard_map/ppermute | solution.py:122
  6.1 56.0 %copy-start.1 = (bf16[128,512]{1,0:T(8,128)(2,1)S(1)}, bf16[128,512]{1,0:T(8,128)(2,1)}, u32[]{:S(2)}) copy-start(bf16[128,512]{1,0:T(8,128)(2,1)} %w_self_ref.1) | copy-start | bytes 393220
  6.1 56.0 %copy-start.2 = (bf16[128,512]{1,0:T(8,128)(2,1)S(1)}, bf16[128,512]{1,0:T(8,128)(2,1)}, u32[]{:S(2)}) copy-start(bf16[128,512]{1,0:T(8,128)(2,1)} %w_neigh_ref.1) | copy-start | bytes 393220
  6.1 56.0 %copy-start.4 = (f32[512]{0:T(512)S(1)}, f32[512]{0:T(512)}, u32[]{:S(2)}) copy-start(f32[512]{0:T(512)} %param.13) | copy-start | bytes 6148

commit v3 on v2

--- a/solution.py
+++ b/solution.py
@@ -1,4 +1,5 @@
 import functools
+import math
 
 import jax
 import jax.numpy as jnp
@@ -8,9 +9,10 @@
 from jax.sharding import Mesh, PartitionSpec as P
 
 YH, X, CORE = 2, 4, 2
+ORDER = ("yl", "z", "yh")
 AXES = ("z", "yh", "x", "core", "yl")
 VMEM = pl.BlockSpec(memory_space=pltpu.VMEM)
-PARAMS = pltpu.CompilerParams(vmem_limit_bytes=32 * 1024 * 1024)
+PARAMS = pltpu.CompilerParams(vmem_limit_bytes=12 * 1024 * 1024)
 
 
 def multiply_half(which, features_ref, adjacency_ref, out_ref):
@@ -26,13 +28,17 @@
     multiply_half(1 - lax.axis_index("core"), features_ref, adjacency_ref, out_ref)
 
 
-def own_kernel(features_ref, adjacency_ref, slot_ref, in_degree_ref, out_ref, select_ref, degree_ref):
+def own_kernel(first, places, features_ref, adjacency_ref, slot_ref, in_degree_ref, w_ref, bias_ref, out_ref, select_ref, degree_ref, own_ref):
     multiply_half(lax.axis_index("core"), features_ref, adjacency_ref, out_ref)
     rows, wide = select_ref.shape
     s, tiles = in_degree_ref.shape
     p = slot_ref.shape[1]
     column = lax.broadcasted_iota(jnp.int32, (p, wide), 1)
-    source = lax.rem(lax.div(column, s), p)
+    message = lax.div(column, s)
+    message = jnp.where(message == 0, first, jnp.where(message <= first, message - 1, message))
+    source = jnp.zeros_like(column)
+    for stride, size, weight in places:
+        source = source + lax.rem(lax.div(message, stride), size) * weight
     spread = (source == lax.broadcasted_iota(jnp.int32, (p, wide), 0)).astype(jnp.float32).astype(jnp.bfloat16)
     slots = slot_ref[...].astype(jnp.float32).astype(jnp.bfloat16)
     slots = jnp.dot(slots, spread, preferred_element_type=jnp.float32).astype(jnp.int32)
@@ -47,6 +53,7 @@
     mine = tile == lax.broadcasted_iota(jnp.int32, (rows, tiles), 1)
     degree = jnp.sum(jnp.where(mine, degrees, 0.0), axis=1, keepdims=True)
     degree_ref[...] = jnp.broadcast_to(degree, degree_ref.shape)
+    own_ref[...] = jnp.dot(features_ref[...].astype(jnp.bfloat16), w_ref[...], preferred_element_type=jnp.float32) + bias_ref[...]
 
 
 def half_call(kernel, operands, extra):
@@ -77,7 +84,7 @@
     )(mine, got)
 
 
-def quad_kernel(s, p, pieces_ref, out_ref, total):
+def quad_kernel(s, p, index, pieces_ref, out_ref, total):
     for b in range(YH):
         for i in range(s):
             at = pl.ds(i * p, p)
@@ -87,13 +94,13 @@
             total[b, at, :] = acc
     for b in range(YH):
         for q in range(p):
-            out_ref[b * p + q] = total[b, pl.ds(q, s, stride=p), :].astype(jnp.bfloat16)
+            out_ref[index(b, q)] = total[b, pl.ds(q, s, stride=p), :].astype(jnp.bfloat16)
 
 
-def quad_sum(pieces, s, p):
+def quad_sum(pieces, s, p, index):
     f = pieces.shape[-1]
     return pl.pallas_call(
-        functools.partial(quad_kernel, s, p),
+        functools.partial(quad_kernel, s, p, index),
         out_shape=jax.ShapeDtypeStruct((YH * p, s, f), jnp.bfloat16),
         in_specs=[VMEM],
         out_specs=VMEM,
@@ -102,15 +109,16 @@
     )(pieces)
 
 
-def final_kernel(select_ref, degree_ref, features_ref, received_ref, w_self_ref, w_neigh_ref, bias_ref, out_ref):
+def final_kernel(select_ref, degree_ref, own_ref, received_ref, w_neigh_ref, out_ref):
     neigh_sum = jnp.dot(select_ref[...], received_ref[...], preferred_element_type=jnp.float32)
     aggregate = (neigh_sum / degree_ref[...]).astype(jnp.bfloat16)
-    hidden = jnp.dot(features_ref[...].astype(jnp.bfloat16), w_self_ref[...], preferred_element_type=jnp.float32)
-    hidden = hidden + jnp.dot(aggregate, w_neigh_ref[...], preferred_element_type=jnp.float32)
-    out_ref[...] = jnp.maximum(hidden + bias_ref[...], 0.0).astype(jnp.bfloat16)
+    hidden = own_ref[...] + jnp.dot(aggregate, w_neigh_ref[...], preferred_element_type=jnp.float32)
+    out_ref[...] = jnp.maximum(hidden, 0.0).astype(jnp.bfloat16)
 
 
 def make_local(z, yl):
+    sizes = {"z": z, "yh": YH, "yl": yl}
+
     def local(features, adjacency, slot_tile, in_degree, w_self, w_neigh, bias):
         tiles, s, f = features.shape
         p = z * yl
@@ -118,23 +126,34 @@
         h = w_self.shape[1]
         node_rows = features.reshape(rows, f).astype(jnp.float32)
         adj = adjacency.reshape(YH, X, CORE, s, p, -1)
+        strides = {name: math.prod(sizes[later] for later in ORDER[k + 1 :]) for k, name in enumerate(ORDER)}
+        first = (2 * z // 3) * strides["z"] + (YH - 1) * strides["yh"]
+        order = [first] + [member for member in range(YH * p) if member != first]
+
+        def index(b, q):
+            member = b * strides["yh"] + (q // yl) * strides["z"] + (q % yl) * strides["yl"]
+            return order.index(member)
+
         (other,) = half_call(other_kernel, (node_rows, adj), [])
         got = lax.ppermute(other, "core", [(0, 1), (1, 0)])
         tables = [
             jax.ShapeDtypeStruct((rows, YH * p * s), jnp.bfloat16),
             jax.ShapeDtypeStruct((rows, f), jnp.float32),
+            jax.ShapeDtypeStruct((rows, h), jnp.float32),
         ]
-        mine, select, degree = half_call(own_kernel, (node_rows, adj, slot_tile, in_degree.T), tables)
+        places = ((strides["z"], z, yl), (strides["yl"], yl, 1))
+        own = functools.partial(own_kernel, first, places)
+        mine, select, degree, own_term = half_call(own, (node_rows, adj, slot_tile, in_degree.T, w_self, bias.reshape(1, h)), tables)
         pair = pair_sum(mine, got)
-        quad = quad_sum(lax.all_to_all(pair, "x", 0, 0, tiled=True), s, p)
-        received = lax.all_to_all(quad, ("yh", "z", "yl"), 0, 0, tiled=True)
+        quad = quad_sum(lax.all_to_all(pair, "x", 0, 0, tiled=True), s, p, index)
+        received = lax.all_to_all(quad, ORDER, 0, 0, tiled=True, axis_index_groups=[order])
         embedding = pl.pallas_call(
             final_kernel,
             out_shape=jax.ShapeDtypeStruct((rows, h), jnp.bfloat16),
-            in_specs=[VMEM] * 7,
+            in_specs=[VMEM] * 5,
             out_specs=VMEM,
             compiler_params=PARAMS,
-        )(select, degree, node_rows, received.reshape(YH * p * s, f), w_self, w_neigh, bias.reshape(1, h))
+        )(select, degree, own_term, received.reshape(YH * p * s, f), w_neigh)
         return embedding.reshape(tiles, s, h)
 
     return local

time: 63.6 us -> 57 us (0.90)
  blocking collectives: 54.2 us -> 47.7 us
    all_to_all x2, blocking collectives: 54.2 us -> 47.7 us  [the longest x1 31 us: local(): lax.all_to_all(quad, ORDER, 0, 0, tiled=True, axis_index_groups=[order])]
where the time goes in v3:
time: 57 us; the launch traced here: 56.8 us
  blocking collectives  47.7 us (84%)
  Pallas kernels  2.87 us (5%)
  starting transfers between devices  1.92 us (3%)
  local copies, waits for them, and re-layouts  1.91 us (3%)
  waiting for transfers between devices  1.38 us (2%)
  other arithmetic  0.89 us (2%)
    all_to_all x1, blocking collectives, local(): lax.all_to_all(quad, ORDER, 0, 0, tiled=True, axis_index_groups=[order])  31 us
    all_to_all x1, blocking collectives, local(): quad = quad_sum(lax.all_to_all(pair, 'x', 0, 0, tiled=True), s, p, index)  16.7 us
    ppermute x1, starting transfers between devices, local(): got = lax.ppermute(other, 'core', [(0, 1), (1, 0)])  1.92 us
    unnamed x12, local copies, waits for them, and re-layouts  1.91 us
    pallas_call x2, Pallas kernels, half_call(): pl.pallas_call(kernel, out_shape=[jax.ShapeDtypeStruct((X, YH, s * p, f),...  1.39 us
    ppermute x1, waiting for transfers between devices, local(): got = lax.ppermute(other, 'core', [(0, 1), (1, 0)])  1.38 us
  transfers between devices with their start and end apart: 1, of which 1 were waited for; matrix products, arithmetic and copies ran while one was open for 0% of the time, Pallas kernels for 1%

profile of v3, /device:TPU:8, one launch (start us, length us, event | category | flops | bytes accessed | tf_op | source)
XLA Modules:
  0.0 56.8 jit_solution(12926549342527941173)
XLA Ops:
  0.0 0.0 copy-start.4
  0.0 0.0 copy-start.1
  0.0 0.0 copy-start.3
  0.0 0.0 copy-start.5
  0.0 0.9 %bitcast_convert_fusion.features_ref = f32[256,128]{1,0:T(8,128)S(1)} fusion(bf16[32,8,128]{2,1,0:T(8,128)(2,1)} %param.7), kind=kLoop, calls=%fused_computation | loop fusion | flops 32768 | bytes 196608 | tf_op jit(solution)/shard_map/convert_element_type | solution.py:127
  0.9 0.0 copy-start
  0.9 1.9 %copy-done = bf16[1,1,128,48,256]{4,3,2,1,0:T(8,128)(2,1)S(1)} copy-done((bf16[1,1,128,48,256]{4,3,2,1,0:T(8,128)(2,1)S(1)}, bf16[1,1,128,48,256]{4,3,2,1,0:T(8,128)(2,1)}, u32[]{:S(2)}) %copy-start) | copy-done | bytes 3145752
  2.8 0.6 %shard_map.74 = bf16[4,2,384,128]{3,2,1,0:T(8,128)(2,1)S(1)} custom-call(f32[256,128]{1,0:T(8,128)S(1)} %bitcast_convert_fusion.features_ref, bf16[2,4,2,8,48,256]{5,4,3,2,1,0:T(8,128)(2,1)S(1)} %bitcast.8), custom_call_target="tpu_custom_call" | custom-call | flops 201326592 | bytes 3000000 | tf_op jit(solution)/shard_map/pallas_call | solution.py:63
  3.4 1.9 %collective-permute-start = (bf16[4,2,384,128]{3,2,1,0:T(8,128)(2,1)S(1)}, bf16[4,2,384,128]{3,2,1,0:T(8,128)(2,1)S(1)}, u32[]{:S(2)}, u32[]{:S(2)}) collective-permute-start(bf16[4,2,384,128]{3,2,1,0:T(8,128)(2,1)S(1)} %shard_map.74), channel_id=1, source_target_pairs={{0,4},{4,0},{1,5},{5,1},{2,6},{6,2},{3,7},{7,3},{8,12},{12,8},{9,1... | collective-permute-start | bytes 2359304 | tf_op jit(solution)/shard_map/ppermute | solution.py:138
  5.3 0.0 copy-done.4
  5.3 0.0 copy-done.1
  5.3 0.0 copy-done.3
  5.3 0.0 copy-done.5
  5.3 0.8 %shard_map.73 = (bf16[4,2,384,128]{3,2,1,0:T(8,128)(2,1)S(1)}, bf16[256,768]{1,0:T(8,128)(2,1)S(1)}, f32[256,128]{1,0:T(8,128)S(1)}, f32[256,512]{1,0:T(8,128)S(1)}) custom-call(f32[256,128]{1,0:T(8,128)S(1)} %bitcast_convert_fusion.features_ref, bf16[2,4,2,8,48,256]{5,4,3,2,1,0:T(8,128)(2,1)S(1)} %bitcast.9, s32[1,48]{1,0:T(1,128)S(1)} %copy-done.5, ...), custom_call_target="tpu_custom_call" | custom-call | flops 201326592 | bytes 3000000 | tf_op jit(solution)/shard_map/pallas_call | solution.py:63
  6.2 0.0 copy-start.2
  6.2 1.4 %collective-permute-done.got_ref = bf16[4,2,384,128]{3,2,1,0:T(8,128)(2,1)S(1)} collective-permute-done((bf16[4,2,384,128]{3,2,1,0:T(8,128)(2,1)S(1)}, bf16[4,2,384,128]{3,2,1,0:T(8,128)(2,1)S(1)}, u32[]{:S(2)}, u32[]{:S(2)}) %collective-permute-start) | collective-permute-done | bytes 786464 | tf_op jit(solution)/shard_map/ppermute | solution.py:138
  7.6 0.2 shard_map.75
  7.7 16.7 %all_to_all.10.pieces_ref = bf16[4,2,384,128]{3,2,1,0:T(8,128)(2,1)S(1)} all-to-all(bf16[4,2,384,128]{3,2,1,0:T(8,128)(2,1)S(1)} %shard_map.75), channel_id=1, replica_groups=mesh['z'=12,'yh'=2,'x'=4,'core'=2,'yl'=4] {'x'}, dimensions={0} | all-to-all | bytes 1572864 | tf_op jit(solution)/shard_map/all_to_all | solution.py:148
  24.4 0.2 shard_map.76
  24.6 31.0 %all_to_all.11 = bf16[96,8,128]{2,1,0:T(8,128)(2,1)S(1)} all-to-all(bf16[96,8,128]{2,1,0:T(8,128)(2,1)S(1)} %shard_map.76), channel_id=1, replica_groups={{544,0,32,64,96,128,160,192,224,256,288,320,352,384,416,448,480,512,576..., dimensions={0} | all-to-all | bytes 393216 | tf_op jit(solution)/shard_map/all_to_all | solution.py:149
  55.7 0.0 copy-done.2
  55.7 1.1 %shard_map.77 = bf16[256,512]{1,0:T(8,128)(2,1)} custom-call(bf16[256,768]{1,0:T(8,128)(2,1)S(1)} %get-tuple-element.9.select_ref, f32[256,128]{1,0:T(8,128)S(1)} %get-tuple-element.10.degree_ref, f32[256,512]{1,0:T(8,128)S(1)} %get-tuple-element.11.own_ref, bf16[768,128]{1,0:T(8,128)(2,1)S(1)} %bitcast.10, bf16[128,512]{1,0:T(8,128)(2,1)S(1)} %copy-done.2), custom_call_target="tpu_custom_call" | custom-call | tf_op jit(solution)/shard_map/pallas_call | solution.py:150
Async XLA Ops:
  0.0 5.3 %copy-start.4 = (f32[512]{0:T(512)S(1)}, f32[512]{0:T(512)}, u32[]{:S(2)}) copy-start(f32[512]{0:T(512)} %param.13) | copy-start | bytes 6148
  0.0 5.3 %copy-start.1 = (bf16[128,512]{1,0:T(8,128)(2,1)S(1)}, bf16[128,512]{1,0:T(8,128)(2,1)}, u32[]{:S(2)}) copy-start(bf16[128,512]{1,0:T(8,128)(2,1)} %w_ref.1) | copy-start | bytes 393220
  0.0 5.3 %copy-start.3 = (s32[32,8]{0,1:T(8,128)S(1)}, s32[32,8]{0,1:T(8,128)}, u32[]{:S(2)}) copy-start(s32[32,8]{0,1:T(8,128)} %param.10) | copy-start | bytes 3076
  0.0 5.3 %copy-start.5 = (s32[1,48]{1,0:T(1,128)S(1)}, s32[1,48]{1,0:T(1,128)}, u32[]{:S(2)}) copy-start(s32[1,48]{1,0:T(1,128)} %slot_ref.1) | copy-start | bytes 580
  0.9 1.9 %copy-start = (bf16[1,1,128,48,256]{4,3,2,1,0:T(8,128)(2,1)S(1)}, bf16[1,1,128,48,256]{4,3,2,1,0:T(8,128)(2,1)}, u32[]{:S(2)}) copy-start(bf16[1,1,128,48,256]{4,3,2,1,0:T(8,128)(2,1)} %param.8) | copy-start | bytes 9437188
  3.4 4.2 %collective-permute-start = (bf16[4,2,384,128]{3,2,1,0:T(8,128)(2,1)S(1)}, bf16[4,2,384,128]{3,2,1,0:T(8,128)(2,1)S(1)}, u32[]{:S(2)}, u32[]{:S(2)}) collective-permute-start(bf16[4,2,384,128]{3,2,1,0:T(8,128)(2,1)S(1)} %shard_map.74), channel_id=1, source_target_pairs={{0,4},{4,0},{1,5},{5,1},{2,6},{6,2},{3,7},{7,3},{8,12},{12,8},{9,1... | collective-permute-start | bytes 2359304 | tf_op jit(solution)/shard_map/ppermute | solution.py:138
  6.2 49.5 %copy-start.2 = (bf16[128,512]{1,0:T(8,128)(2,1)S(1)}, bf16[128,512]{1,0:T(8,128)(2,1)}, u32[]{:S(2)}) copy-start(bf16[128,512]{1,0:T(8,128)(2,1)} %w_neigh_ref.1) | copy-start | bytes 393220

commit v4 on v3

--- a/solution.py
+++ b/solution.py
@@ -17,14 +17,28 @@
 
 def multiply_half(which, features_ref, adjacency_ref, out_ref):
     s, p, c = adjacency_ref.shape[3:]
-    right = features_ref[...].astype(jnp.bfloat16)
+    right = features_ref[...]
     for a in range(X):
         for b in range(YH):
             left = adjacency_ref[b, a, which].reshape(s * p, c)
-            out_ref[a, b] = jnp.dot(left, right, preferred_element_type=jnp.float32).astype(jnp.bfloat16)
+            out_ref[(a + X // 2) % X, b] = jnp.dot(left, right, preferred_element_type=jnp.float32).astype(jnp.bfloat16)
 
 
-def other_kernel(features_ref, adjacency_ref, out_ref):
+def mark_kernel(out_ref):
+    out_ref[...] = jnp.zeros_like(out_ref)
+
+
+def mark_call():
+    return pl.pallas_call(
+        mark_kernel,
+        out_shape=jax.ShapeDtypeStruct((8, 128), jnp.float32),
+        out_specs=VMEM,
+        compiler_params=PARAMS,
+        cost_estimate=pl.CostEstimate(flops=4000000000, bytes_accessed=4096, transcendentals=0),
+    )()
+
+
+def other_kernel(features_ref, adjacency_ref, mark_ref, out_ref):
     multiply_half(1 - lax.axis_index("core"), features_ref, adjacency_ref, out_ref)
 
 
@@ -53,7 +67,7 @@
     mine = tile == lax.broadcasted_iota(jnp.int32, (rows, tiles), 1)
     degree = jnp.sum(jnp.where(mine, degrees, 0.0), axis=1, keepdims=True)
     degree_ref[...] = jnp.broadcast_to(degree, degree_ref.shape)
-    own_ref[...] = jnp.dot(features_ref[...].astype(jnp.bfloat16), w_ref[...], preferred_element_type=jnp.float32) + bias_ref[...]
+    own_ref[...] = jnp.dot(features_ref[...], w_ref[...], preferred_element_type=jnp.float32) + bias_ref[...]
 
 
 def half_call(kernel, operands, extra):
@@ -124,7 +138,7 @@
         p = z * yl
         rows = tiles * s
         h = w_self.shape[1]
-        node_rows = features.reshape(rows, f).astype(jnp.float32)
+        node_rows = features.reshape(rows, f)
         adj = adjacency.reshape(YH, X, CORE, s, p, -1)
         strides = {name: math.prod(sizes[later] for later in ORDER[k + 1 :]) for k, name in enumerate(ORDER)}
         first = (2 * z // 3) * strides["z"] + (YH - 1) * strides["yh"]
@@ -134,7 +148,7 @@
             member = b * strides["yh"] + (q // yl) * strides["z"] + (q % yl) * strides["yl"]
             return order.index(member)
 
-        (other,) = half_call(other_kernel, (node_rows, adj), [])
+        (other,) = half_call(other_kernel, (node_rows, adj, mark_call()), [])
         got = lax.ppermute(other, "core", [(0, 1), (1, 0)])
         tables = [
             jax.ShapeDtypeStruct((rows, YH * p * s), jnp.bfloat16),
@@ -144,8 +158,9 @@
         places = ((strides["z"], z, yl), (strides["yl"], yl, 1))
         own = functools.partial(own_kernel, first, places)
         mine, select, degree, own_term = half_call(own, (node_rows, adj, slot_tile, in_degree.T, w_self, bias.reshape(1, h)), tables)
+        columns = [(k + X // 2) % X for k in range(X)]
         pair = pair_sum(mine, got)
-        quad = quad_sum(lax.all_to_all(pair, "x", 0, 0, tiled=True), s, p, index)
+        quad = quad_sum(lax.all_to_all(pair, "x", 0, 0, tiled=True, axis_index_groups=[columns]), s, p, index)
         received = lax.all_to_all(quad, ORDER, 0, 0, tiled=True, axis_index_groups=[order])
         embedding = pl.pallas_call(
             final_kernel,

time: 57 us -> 55.8 us (0.979)
  the two profiles are of different devices: /device:TPU:8 before, /device:TPU:4 now
where the time goes in v4:
time: 55.8 us; the launch traced here: 55.6 us
  blocking collectives  47.4 us (85%)
  Pallas kernels  2.97 us (5%)
  starting transfers between devices  1.92 us (3%)
  local copies, waits for them, and re-layouts  1.87 us (3%)
  waiting for transfers between devices  1.38 us (2%)
    all_to_all x1, blocking collectives, local(): lax.all_to_all(quad, ORDER, 0, 0, tiled=True, axis_index_groups=[order])  24.2 us
    all_to_all x1, blocking collectives, local(): lax.all_to_all(pair, 'x', 0, 0, tiled=True, axis_index_groups=[columns])  23.2 us
    ppermute x1, starting transfers between devices, local(): got = lax.ppermute(other, 'core', [(0, 1), (1, 0)])  1.92 us
    unnamed x14, local copies, waits for them, and re-layouts  1.87 us
    pallas_call x2, Pallas kernels, half_call(): pl.pallas_call(kernel, out_shape=[jax.ShapeDtypeStruct((X, YH, s * p, f),...  1.39 us
    ppermute x1, waiting for transfers between devices, local(): got = lax.ppermute(other, 'core', [(0, 1), (1, 0)])  1.38 us
  transfers between devices with their start and end apart: 1, of which 1 were waited for; matrix products, arithmetic and copies ran while one was open for 0% of the time, Pallas kernels for 1%

profile of v4, /device:TPU:4, one launch (start us, length us, event | category | flops | bytes accessed | tf_op | source)
XLA Modules:
  0.0 55.6 jit_solution(15267962828202118933)
XLA Ops:
  0.0 0.0 copy-start
  0.0 0.0 copy-start.1
  0.0 0.0 copy-start.2
  0.0 0.0 copy-start.4
  0.0 0.0 copy-start.5
  0.0 0.0 copy-start.6
  0.1 1.8 %copy-done = bf16[1,1,128,48,256]{4,3,2,1,0:T(8,128)(2,1)S(1)} copy-done((bf16[1,1,128,48,256]{4,3,2,1,0:T(8,128)(2,1)S(1)}, bf16[1,1,128,48,256]{4,3,2,1,0:T(8,128)(2,1)}, u32[]{:S(2)}) %copy-start) | copy-done | bytes 3145752
  1.9 0.0 copy-done.1
  1.9 0.6 %shard_map.75 = bf16[4,2,384,128]{3,2,1,0:T(8,128)(2,1)S(1)} custom-call(bf16[256,128]{1,0:T(8,128)(2,1)S(1)} %bitcast.9, bf16[2,4,2,8,48,256]{5,4,3,2,1,0:T(8,128)(2,1)S(1)} %bitcast.6, f32[8,128]{1,0:T(8,128)S(1)} %shard_map.74.mark_ref), custom_call_target="tpu_custom_call" | custom-call | flops 201326592 | bytes 3000000 | tf_op jit(solution)/shard_map/pallas_call | solution.py:77
  2.5 1.9 %collective-permute-start = (bf16[4,2,384,128]{3,2,1,0:T(8,128)(2,1)S(1)}, bf16[4,2,384,128]{3,2,1,0:T(8,128)(2,1)S(1)}, u32[]{:S(2)}, u32[]{:S(2)}) collective-permute-start(bf16[4,2,384,128]{3,2,1,0:T(8,128)(2,1)S(1)} %shard_map.75), channel_id=1, source_target_pairs={{0,4},{4,0},{1,5},{5,1},{2,6},{6,2},{3,7},{7,3},{8,12},{12,8},{9,1... | collective-permute-start | bytes 2359304 | tf_op jit(solution)/shard_map/ppermute | solution.py:152
  4.4 0.0 copy-done.2
  4.4 0.0 copy-done.4
  4.4 0.0 copy-done.5
  4.4 0.0 copy-done.6
  4.4 0.8 %shard_map.73 = (bf16[4,2,384,128]{3,2,1,0:T(8,128)(2,1)S(1)}, bf16[256,768]{1,0:T(8,128)(2,1)S(1)}, f32[256,128]{1,0:T(8,128)S(1)}, f32[256,512]{1,0:T(8,128)S(1)}) custom-call(bf16[256,128]{1,0:T(8,128)(2,1)S(1)} %bitcast.10, bf16[2,4,2,8,48,256]{5,4,3,2,1,0:T(8,128)(2,1)S(1)} %bitcast.7, s32[1,48]{1,0:T(1,128)S(1)} %copy-done.6, s32[8,32]{1,0:T(8,128)S(1)} %bitcast.11, ...), custom_call_target="tpu_custom_call" | custom-call | flops 201326592 | bytes 3000000 | tf_op jit(solution)/shard_map/pallas_call | solution.py:77
  5.3 0.0 copy-start.3
  5.3 1.4 %collective-permute-done.got_ref = bf16[4,2,384,128]{3,2,1,0:T(8,128)(2,1)S(1)} collective-permute-done((bf16[4,2,384,128]{3,2,1,0:T(8,128)(2,1)S(1)}, bf16[4,2,384,128]{3,2,1,0:T(8,128)(2,1)S(1)}, u32[]{:S(2)}, u32[]{:S(2)}) %collective-permute-start) | collective-permute-done | bytes 786464 | tf_op jit(solution)/shard_map/ppermute | solution.py:152
  6.6 0.3 shard_map.76
  6.9 23.2 %all_to_all.10.pieces_ref = bf16[4,2,384,128]{3,2,1,0:T(8,128)(2,1)S(1)} all-to-all(bf16[4,2,384,128]{3,2,1,0:T(8,128)(2,1)S(1)} %shard_map.76), channel_id=1, replica_groups={{16,24,0,8},{17,25,1,9},{18,26,2,10},{19,27,3,11},{20,28,4,12},{21,29,5..., dimensions={0} | all-to-all | bytes 1572864 | tf_op jit(solution)/shard_map/all_to_all | solution.py:163
  30.1 0.2 shard_map.77
  30.3 24.2 %all_to_all.11 = bf16[96,8,128]{2,1,0:T(8,128)(2,1)S(1)} all-to-all(bf16[96,8,128]{2,1,0:T(8,128)(2,1)S(1)} %shard_map.77), channel_id=1, replica_groups={{544,0,32,64,96,128,160,192,224,256,288,320,352,384,416,448,480,512,576..., dimensions={0} | all-to-all | bytes 393216 | tf_op jit(solution)/shard_map/all_to_all | solution.py:164
  54.5 0.0 copy-done.3
  54.5 1.1 %shard_map.78 = bf16[256,512]{1,0:T(8,128)(2,1)} custom-call(bf16[256,768]{1,0:T(8,128)(2,1)S(1)} %get-tuple-element.9.select_ref, f32[256,128]{1,0:T(8,128)S(1)} %get-tuple-element.10.degree_ref, f32[256,512]{1,0:T(8,128)S(1)} %get-tuple-element.11.own_ref, bf16[768,128]{1,0:T(8,128)(2,1)S(1)} %bitcast.8, bf16[128,512]{1,0:T(8,128)(2,1)S(1)} %copy-done.3), custom_call_target="tpu_custom_call" | custom-call | tf_op jit(solution)/shard_map/pallas_call | solution.py:165
  (1 shorter events, 0.0 us)
Async XLA Ops:
  0.0 1.9 %copy-start = (bf16[1,1,128,48,256]{4,3,2,1,0:T(8,128)(2,1)S(1)}, bf16[1,1,128,48,256]{4,3,2,1,0:T(8,128)(2,1)}, u32[]{:S(2)}) copy-start(bf16[1,1,128,48,256]{4,3,2,1,0:T(8,128)(2,1)} %param.8) | copy-start | bytes 9437188
  0.0 1.9 %copy-start.1 = (bf16[32,8,128]{2,1,0:T(8,128)(2,1)S(1)}, bf16[32,8,128]{2,1,0:T(8,128)(2,1)}, u32[]{:S(2)}) copy-start(bf16[32,8,128]{2,1,0:T(8,128)(2,1)} %param.7) | copy-start | bytes 196612
  0.0 4.4 %copy-start.2 = (bf16[128,512]{1,0:T(8,128)(2,1)S(1)}, bf16[128,512]{1,0:T(8,128)(2,1)}, u32[]{:S(2)}) copy-start(bf16[128,512]{1,0:T(8,128)(2,1)} %w_ref.1) | copy-start | bytes 393220
  0.0 4.4 %copy-start.4 = (s32[32,8]{0,1:T(8,128)S(1)}, s32[32,8]{0,1:T(8,128)}, u32[]{:S(2)}) copy-start(s32[32,8]{0,1:T(8,128)} %param.10) | copy-start | bytes 3076
  0.0 4.4 %copy-start.5 = (f32[512]{0:T(512)S(1)}, f32[512]{0:T(512)}, u32[]{:S(2)}) copy-start(f32[512]{0:T(512)} %param.13) | copy-start | bytes 6148
  0.0 4.4 %copy-start.6 = (s32[1,48]{1,0:T(1,128)S(1)}, s32[1,48]{1,0:T(1,128)}, u32[]{:S(2)}) copy-start(s32[1,48]{1,0:T(1,128)} %slot_ref.1) | copy-start | bytes 580
  2.5 4.2 %collective-permute-start = (bf16[4,2,384,128]{3,2,1,0:T(8,128)(2,1)S(1)}, bf16[4,2,384,128]{3,2,1,0:T(8,128)(2,1)S(1)}, u32[]{:S(2)}, u32[]{:S(2)}) collective-permute-start(bf16[4,2,384,128]{3,2,1,0:T(8,128)(2,1)S(1)} %shard_map.75), channel_id=1, source_target_pairs={{0,4},{4,0},{1,5},{5,1},{2,6},{6,2},{3,7},{7,3},{8,12},{12,8},{9,1... | collective-permute-start | bytes 2359304 | tf_op jit(solution)/shard_map/ppermute | solution.py:152
  5.3 49.3 %copy-start.3 = (bf16[128,512]{1,0:T(8,128)(2,1)S(1)}, bf16[128,512]{1,0:T(8,128)(2,1)}, u32[]{:S(2)}) copy-start(bf16[128,512]{1,0:T(8,128)(2,1)} %w_neigh_ref.1) | copy-start | bytes 393220

commit v5 on v4

--- a/solution.py
+++ b/solution.py
@@ -66,7 +66,7 @@
     tile = lax.div(lax.broadcasted_iota(jnp.int32, (rows, tiles), 0), s)
     mine = tile == lax.broadcasted_iota(jnp.int32, (rows, tiles), 1)
     degree = jnp.sum(jnp.where(mine, degrees, 0.0), axis=1, keepdims=True)
-    degree_ref[...] = jnp.broadcast_to(degree, degree_ref.shape)
+    degree_ref[...] = jnp.broadcast_to(1.0 / degree, degree_ref.shape)
     own_ref[...] = jnp.dot(features_ref[...], w_ref[...], preferred_element_type=jnp.float32) + bias_ref[...]
 
 
@@ -82,20 +82,6 @@
         compiler_params=PARAMS,
         cost_estimate=pl.CostEstimate(flops=X * YH * s * p * c * f * 2, bytes_accessed=3000000, transcendentals=0),
     )(*operands)
-
-
-def pair_kernel(mine_ref, got_ref, out_ref):
-    out_ref[...] = mine_ref[...] + got_ref[...]
-
-
-def pair_sum(mine, got):
-    return pl.pallas_call(
-        pair_kernel,
-        out_shape=jax.ShapeDtypeStruct(mine.shape, jnp.bfloat16),
-        in_specs=[VMEM, VMEM],
-        out_specs=VMEM,
-        compiler_params=PARAMS,
-    )(mine, got)
 
 
 def quad_kernel(s, p, index, pieces_ref, out_ref, total):
@@ -125,7 +111,7 @@
 
 def final_kernel(select_ref, degree_ref, own_ref, received_ref, w_neigh_ref, out_ref):
     neigh_sum = jnp.dot(select_ref[...], received_ref[...], preferred_element_type=jnp.float32)
-    aggregate = (neigh_sum / degree_ref[...]).astype(jnp.bfloat16)
+    aggregate = (neigh_sum * degree_ref[...]).astype(jnp.bfloat16)
     hidden = own_ref[...] + jnp.dot(aggregate, w_neigh_ref[...], preferred_element_type=jnp.float32)
     out_ref[...] = jnp.maximum(hidden, 0.0).astype(jnp.bfloat16)
 
@@ -159,7 +145,7 @@
         own = functools.partial(own_kernel, first, places)
         mine, select, degree, own_term = half_call(own, (node_rows, adj, slot_tile, in_degree.T, w_self, bias.reshape(1, h)), tables)
         columns = [(k + X // 2) % X for k in range(X)]
-        pair = pair_sum(mine, got)
+        pair = mine + got
         quad = quad_sum(lax.all_to_all(pair, "x", 0, 0, tiled=True, axis_index_groups=[columns]), s, p, index)
         received = lax.all_to_all(quad, ORDER, 0, 0, tiled=True, axis_index_groups=[order])
         embedding = pl.pallas_call(

time: 55.8 us -> 55.8 us (level)
  no operation moved by 1% of the time
where the time goes in v5:
time: 55.8 us; the launch traced here: 55.6 us
  blocking collectives  47.4 us (85%)
  Pallas kernels  2.7 us (5%)
  starting transfers between devices  1.92 us (3%)
  local copies, waits for them, and re-layouts  1.87 us (3%)
  waiting for transfers between devices  1.37 us (2%)
    all_to_all x1, blocking collectives, local(): lax.all_to_all(quad, ORDER, 0, 0, tiled=True, axis_index_groups=[order])  24.2 us
    all_to_all x1, blocking collectives, local(): lax.all_to_all(pair, 'x', 0, 0, tiled=True, axis_index_groups=[columns])  23.2 us
    ppermute x1, starting transfers between devices, local(): got = lax.ppermute(other, 'core', [(0, 1), (1, 0)])  1.92 us
    unnamed x14, local copies, waits for them, and re-layouts  1.87 us
    pallas_call x2, Pallas kernels, half_call(): pl.pallas_call(kernel, out_shape=[jax.ShapeDtypeStruct((X, YH, s * p, f),...  1.39 us
    ppermute x1, waiting for transfers between devices, local(): got = lax.ppermute(other, 'core', [(0, 1), (1, 0)])  1.37 us
  transfers between devices with their start and end apart: 1, of which 1 were waited for; matrix products, arithmetic and copies ran while one was open for 0% of the time, Pallas kernels for 1%

profile of v5, /device:TPU:4, one launch (start us, length us, event | category | flops | bytes accessed | tf_op | source)
XLA Modules:
  0.0 55.6 jit_solution(16192821137734131962)
XLA Ops:
  0.0 0.0 copy-start
  0.0 0.0 copy-start.1
  0.0 0.0 copy-start.2
  0.0 0.0 copy-start.4
  0.0 0.0 copy-start.5
  0.0 0.0 copy-start.6
  0.1 1.8 %copy-done = bf16[1,1,128,48,256]{4,3,2,1,0:T(8,128)(2,1)S(1)} copy-done((bf16[1,1,128,48,256]{4,3,2,1,0:T(8,128)(2,1)S(1)}, bf16[1,1,128,48,256]{4,3,2,1,0:T(8,128)(2,1)}, u32[]{:S(2)}) %copy-start) | copy-done | bytes 3145752
  1.9 0.0 copy-done.1
  1.9 0.6 %shard_map.75 = bf16[4,2,384,128]{3,2,1,0:T(8,128)(2,1)S(1)} custom-call(bf16[256,128]{1,0:T(8,128)(2,1)S(1)} %bitcast.9, bf16[2,4,2,8,48,256]{5,4,3,2,1,0:T(8,128)(2,1)S(1)} %bitcast.6, f32[8,128]{1,0:T(8,128)S(1)} %shard_map.74.mark_ref), custom_call_target="tpu_custom_call" | custom-call | flops 201326592 | bytes 3000000 | tf_op jit(solution)/shard_map/pallas_call | solution.py:77
  2.5 1.9 %collective-permute-start = (bf16[4,2,384,128]{3,2,1,0:T(8,128)(2,1)S(1)}, bf16[4,2,384,128]{3,2,1,0:T(8,128)(2,1)S(1)}, u32[]{:S(2)}, u32[]{:S(2)}) collective-permute-start(bf16[4,2,384,128]{3,2,1,0:T(8,128)(2,1)S(1)} %shard_map.75), channel_id=1, source_target_pairs={{0,4},{4,0},{1,5},{5,1},{2,6},{6,2},{3,7},{7,3},{8,12},{12,8},{9,1... | collective-permute-start | bytes 2359304 | tf_op jit(solution)/shard_map/ppermute | solution.py:138
  4.4 0.0 copy-done.2
  4.4 0.0 copy-done.4
  4.4 0.0 copy-done.5
  4.4 0.0 copy-done.6
  4.4 0.8 %shard_map.73 = (bf16[4,2,384,128]{3,2,1,0:T(8,128)(2,1)S(1)}, bf16[256,768]{1,0:T(8,128)(2,1)S(1)}, f32[256,128]{1,0:T(8,128)S(1)}, f32[256,512]{1,0:T(8,128)S(1)}) custom-call(bf16[256,128]{1,0:T(8,128)(2,1)S(1)} %bitcast.10, bf16[2,4,2,8,48,256]{5,4,3,2,1,0:T(8,128)(2,1)S(1)} %bitcast.7, s32[1,48]{1,0:T(1,128)S(1)} %copy-done.6, s32[8,32]{1,0:T(8,128)S(1)} %bitcast.11, ...), custom_call_target="tpu_custom_call" | custom-call | flops 201326592 | bytes 3000000 | tf_op jit(solution)/shard_map/pallas_call | solution.py:77
  5.3 0.0 copy-start.3
  5.3 1.4 %collective-permute-done = bf16[4,2,384,128]{3,2,1,0:T(8,128)(2,1)S(1)} collective-permute-done((bf16[4,2,384,128]{3,2,1,0:T(8,128)(2,1)S(1)}, bf16[4,2,384,128]{3,2,1,0:T(8,128)(2,1)S(1)}, u32[]{:S(2)}, u32[]{:S(2)}) %collective-permute-start) | collective-permute-done | bytes 786464 | tf_op jit(solution)/shard_map/ppermute | solution.py:138
  6.6 0.2 add.3
  6.9 23.2 %all_to_all.10.pieces_ref = bf16[4,2,384,128]{3,2,1,0:T(8,128)(2,1)S(1)} all-to-all(bf16[4,2,384,128]{3,2,1,0:T(8,128)(2,1)S(1)} %add.3), channel_id=1, replica_groups={{16,24,0,8},{17,25,1,9},{18,26,2,10},{19,27,3,11},{20,28,4,12},{21,29,5..., dimensions={0} | all-to-all | bytes 1572864 | tf_op jit(solution)/shard_map/all_to_all | solution.py:149
  30.0 0.2 shard_map.76
  30.2 24.2 %all_to_all.11 = bf16[96,8,128]{2,1,0:T(8,128)(2,1)S(1)} all-to-all(bf16[96,8,128]{2,1,0:T(8,128)(2,1)S(1)} %shard_map.76), channel_id=1, replica_groups={{544,0,32,64,96,128,160,192,224,256,288,320,352,384,416,448,480,512,576..., dimensions={0} | all-to-all | bytes 393216 | tf_op jit(solution)/shard_map/all_to_all | solution.py:150
  54.5 0.0 copy-done.3
  54.5 1.1 %shard_map.77 = bf16[256,512]{1,0:T(8,128)(2,1)} custom-call(bf16[256,768]{1,0:T(8,128)(2,1)S(1)} %get-tuple-element.9.select_ref, f32[256,128]{1,0:T(8,128)S(1)} %get-tuple-element.10.degree_ref, f32[256,512]{1,0:T(8,128)S(1)} %get-tuple-element.11.own_ref, bf16[768,128]{1,0:T(8,128)(2,1)S(1)} %bitcast.8, bf16[128,512]{1,0:T(8,128)(2,1)S(1)} %copy-done.3), custom_call_target="tpu_custom_call" | custom-call | tf_op jit(solution)/shard_map/pallas_call | solution.py:151
  (1 shorter events, 0.0 us)
Async XLA Ops:
  0.0 1.9 %copy-start = (bf16[1,1,128,48,256]{4,3,2,1,0:T(8,128)(2,1)S(1)}, bf16[1,1,128,48,256]{4,3,2,1,0:T(8,128)(2,1)}, u32[]{:S(2)}) copy-start(bf16[1,1,128,48,256]{4,3,2,1,0:T(8,128)(2,1)} %param.8) | copy-start | bytes 9437188
  0.0 1.9 %copy-start.1 = (bf16[32,8,128]{2,1,0:T(8,128)(2,1)S(1)}, bf16[32,8,128]{2,1,0:T(8,128)(2,1)}, u32[]{:S(2)}) copy-start(bf16[32,8,128]{2,1,0:T(8,128)(2,1)} %param.7) | copy-start | bytes 196612
  0.0 4.4 %copy-start.2 = (bf16[128,512]{1,0:T(8,128)(2,1)S(1)}, bf16[128,512]{1,0:T(8,128)(2,1)}, u32[]{:S(2)}) copy-start(bf16[128,512]{1,0:T(8,128)(2,1)} %w_ref.1) | copy-start | bytes 393220
  0.0 4.4 %copy-start.4 = (s32[32,8]{0,1:T(8,128)S(1)}, s32[32,8]{0,1:T(8,128)}, u32[]{:S(2)}) copy-start(s32[32,8]{0,1:T(8,128)} %param.10) | copy-start | bytes 3076
  0.0 4.4 %copy-start.5 = (f32[512]{0:T(512)S(1)}, f32[512]{0:T(512)}, u32[]{:S(2)}) copy-start(f32[512]{0:T(512)} %param.13) | copy-start | bytes 6148
  0.0 4.4 %copy-start.6 = (s32[1,48]{1,0:T(1,128)S(1)}, s32[1,48]{1,0:T(1,128)}, u32[]{:S(2)}) copy-start(s32[1,48]{1,0:T(1,128)} %slot_ref.1) | copy-start | bytes 580
  2.5 4.2 %collective-permute-start = (bf16[4,2,384,128]{3,2,1,0:T(8,128)(2,1)S(1)}, bf16[4,2,384,128]{3,2,1,0:T(8,128)(2,1)S(1)}, u32[]{:S(2)}, u32[]{:S(2)}) collective-permute-start(bf16[4,2,384,128]{3,2,1,0:T(8,128)(2,1)S(1)} %shard_map.75), channel_id=1, source_target_pairs={{0,4},{4,0},{1,5},{5,1},{2,6},{6,2},{3,7},{7,3},{8,12},{12,8},{9,1... | collective-permute-start | bytes 2359304 | tf_op jit(solution)/shard_map/ppermute | solution.py:138
  5.3 49.2 %copy-start.3 = (bf16[128,512]{1,0:T(8,128)(2,1)S(1)}, bf16[128,512]{1,0:T(8,128)(2,1)}, u32[]{:S(2)}) copy-start(bf16[128,512]{1,0:T(8,128)(2,1)} %w_neigh_ref.1) | copy-start | bytes 393220
